TPU v7x, 32 devices: a whole 2x2x4 slice. The times are simulated.
32 devices in a mesh: dp: 16 (over z, y, core), tensor: 2 (over x).
Axes of the slice: x: 2, y: 2, z: 4, core: 2. Of those that a mesh axis runs over, the one named last changes fastest.
Arguments:
- cand_ids: int32 [8192], P('dp'), may hold values from 0 to 128001, as said below
- val_ids: int32 [1024], P('dp'), may hold values from 0 to 128001, as said below
- inputs: bfloat16 [8192, 8192], P('dp', 'tensor'), may hold values from -6 to 6
- cotangent: bfloat16 [8192, 8192], P('dp'), may hold values from -6 to 6
- queries: bfloat16 [8192, 8192], P('dp', 'tensor'), may hold values from -16 to 16
- key_rows: bfloat16 [8192, 1024], P('dp', 'tensor'), may hold values from -16 to 16
- value_rows: bfloat16 [8192, 1024], P('dp', 'tensor'), may hold values from -6 to 6
- out_weight: bfloat16 [8192, 8192], P('tensor', 'dp'), may hold values from -0.0625 to 0.0625
- val_inputs: bfloat16 [1024, 8192], P('dp', 'tensor'), may hold values from -6 to 6
- val_cotangents: bfloat16 [1024, 8192], P('dp', 'tensor'), may hold values from -6 to 6
- val_attention: bfloat16 [1024, 8192], P('dp', 'tensor'), may hold values from -6 to 6
- val_query_grads: bfloat16 [1024, 8192], P('dp', 'tensor'), may hold values from -6 to 6
- val_keyvalue_grads: bfloat16 [1024, 2048], P('dp', 'tensor'), may hold values from -6 to 6
Outputs:
- scores: float32 [32, 4], P('dp')
Inputs may be any that keep to these rules, and one draw needn't show every extreme that they name: `cand_ids`: each aligned run of 256 ids is one sequence: ids below 128001, then the padding id 128001 on at most 128 trailing positions. `val_ids`: each aligned run of 256 ids is one sequence: ids below 128001, then the padding id 128001 on at most 128 trailing positions.
All inputs are finite; a program needn't handle non-finite values.
Results may differ from a plain program's by a relative error of at most 0.02.
Values may be sent and summed in bfloat16 or wider, within the bound.
A program may use at most 256 MiB of HBM per device.

v0:
```python
import math

import jax
import jax.numpy as jnp
from jax import lax
from jax.sharding import PartitionSpec as P

D = 8192
HEADS = 64
KV = 8
HD = 128
LEN = 256
VALS = 4


pad_token = 128001
rope_base = 500000.0


def rotation(seq_len, head_width):
    half_dim = head_width // 2
    inv_freq = rope_base ** (-(jnp.arange(half_dim).astype(jnp.float32) * 2.0 / head_width))
    angles = jnp.arange(seq_len).astype(jnp.float32)[:, None] * inv_freq[None, :]
    angles = jnp.concatenate([angles, angles], axis=1)
    return (jnp.cos(angles), jnp.sin(angles))


def turn_half(features):
    half_dim = features.shape[-1] // 2
    return jnp.concatenate([-features[..., half_dim:], features[..., :half_dim]], axis=-1)


def outer_rows(left, right):
    return lax.dot_general(
        left, right, (((1,), (1,)), ((), ())), preferred_element_type=jnp.float32
    )


def sequence_pass(query_raw, key_raw, value_part, grad_out):
    seq_len, head_width = (key_raw.shape[1], key_raw.shape[-1])
    cos_table, sine_table = rotation(seq_len, head_width)
    score_scale = 1.0 / math.sqrt(head_width)
    q_cos = cos_table[None, :, None, None, :]
    q_sine = sine_table[None, :, None, None, :]
    k_cos = cos_table[None, :, None, :]
    k_sine = sine_table[None, :, None, :]
    q_float = query_raw.astype(jnp.float32)
    k_float = key_raw.astype(jnp.float32)
    query_rot = (q_float * q_cos + turn_half(q_float) * q_sine).astype(jnp.bfloat16)
    key_rot = (k_float * k_cos + turn_half(k_float) * k_sine).astype(jnp.bfloat16)
    logits = (
        jnp.einsum("slkgd,smkd->skglm", query_rot, key_rot, preferred_element_type=jnp.float32)
        * score_scale
    )
    allowed = jnp.arange(seq_len)[None, :] <= jnp.arange(seq_len)[:, None]
    logits = jnp.where(allowed, logits, -jnp.inf)
    row_max = jnp.max(logits, axis=-1, keepdims=True)
    raised = jnp.exp(logits - row_max)
    attn_probs = raised / jnp.sum(raised, axis=-1, keepdims=True)
    probs_low = attn_probs.astype(jnp.bfloat16)
    attended = jnp.einsum(
        "skglm,smkd->slkgd", probs_low, value_part, preferred_element_type=jnp.float32
    ).astype(jnp.bfloat16)
    prob_grad = jnp.einsum(
        "slkgd,smkd->skglm", grad_out, value_part, preferred_element_type=jnp.float32
    )
    row_delta = jnp.sum(attn_probs * prob_grad, axis=-1, keepdims=True)
    logit_grad = (attn_probs * (prob_grad - row_delta) * score_scale).astype(jnp.bfloat16)
    dquery = jnp.einsum(
        "skglm,smkd->slkgd", logit_grad, key_rot, preferred_element_type=jnp.float32
    )
    key_grad = jnp.einsum(
        "skglm,slkgd->smkd", logit_grad, query_rot, preferred_element_type=jnp.float32
    )
    dvalue = jnp.einsum(
        "skglm,slkgd->smkd", probs_low, grad_out, preferred_element_type=jnp.float32
    )
    dquery_raw = (dquery * q_cos - turn_half(dquery) * q_sine).astype(jnp.bfloat16)
    dkey_raw = (key_grad * k_cos - turn_half(key_grad) * k_sine).astype(jnp.bfloat16)
    return (attended, dquery_raw, jnp.stack([dkey_raw, dvalue.astype(jnp.bfloat16)], axis=3))


def shards(
    cand_ids,
    val_ids,
    inputs,
    cotangent,
    queries,
    key_rows,
    value_rows,
    out_weight,
    val_inputs,
    val_cotangents,
    val_attention,
    val_query_grads,
    val_keyvalue_grads,
):
    tok_rows = cotangent.shape[0]
    seq_count = tok_rows // LEN
    kv_local = key_rows.shape[1] // HD
    head_group = HEADS // KV
    live_rows = (cand_ids != pad_token).astype(jnp.float32)[:, None]
    masked = (cotangent.astype(jnp.float32) * live_rows).astype(jnp.bfloat16)
    grad_attn = outer_rows(masked, lax.all_gather(out_weight, "dp", axis=1, tiled=True)).astype(
        jnp.bfloat16
    )
    q_shape = (seq_count, LEN, kv_local, head_group, HD)
    kv_shape = (seq_count, LEN, kv_local, HD)
    attended, dquery, kv_grads = sequence_pass(
        queries.reshape(q_shape),
        key_rows.reshape(kv_shape),
        value_rows.reshape(kv_shape),
        grad_attn.reshape(q_shape),
    )
    attended = attended.reshape(tok_rows, -1)
    dquery = dquery.reshape(tok_rows, -1)
    kv_grads = kv_grads.reshape(tok_rows, -1)
    feat_block = val_cotangents.shape[1]
    own_cotangent = lax.dynamic_slice_in_dim(
        masked, lax.axis_index("tensor") * feat_block, feat_block, 1
    )
    val_live = (val_ids != pad_token).astype(jnp.float32)[:, None]
    val_dy = (val_cotangents.astype(jnp.float32) * val_live).astype(jnp.bfloat16)
    val_dq = (val_query_grads.astype(jnp.float32) * val_live).astype(jnp.bfloat16)
    val_dkv = (val_keyvalue_grads.astype(jnp.float32) * val_live).astype(jnp.bfloat16)

    def gram_stack(part_x, part_dy, part_attn, part_dq, part_dkv):
        return jnp.stack(
            [
                outer_rows(attended, part_attn),
                outer_rows(own_cotangent, part_dy),
                outer_rows(inputs, part_x),
                outer_rows(dquery, part_dq) + outer_rows(kv_grads, part_dkv),
            ]
        )

    gathered = (
        lax.all_gather(val_inputs, "dp", axis=0, tiled=True),
        lax.all_gather(val_dy, "dp", axis=0, tiled=True),
        lax.all_gather(val_attention, "dp", axis=0, tiled=True),
        lax.all_gather(val_dq, "dp", axis=0, tiled=True),
        lax.all_gather(val_dkv, "dp", axis=0, tiled=True),
    )
    gram_parts = gram_stack(*gathered)
    factor = 1.0 / (64.0 * D)
    gram_share = lax.psum_scatter(
        gram_parts.astype(jnp.bfloat16), "tensor", scatter_dimension=2, tiled=True
    ).astype(jnp.float32)
    product = gram_share[0] * gram_share[1] + gram_share[2] * gram_share[3]
    col_width = product.shape[1]
    by_seq = jnp.sum(product.reshape(seq_count, LEN, col_width), axis=1)
    column = lax.axis_index("tensor") * col_width + jnp.arange(col_width)
    member = ((column // LEN)[:, None] == jnp.arange(VALS)[None, :]).astype(jnp.float32)
    partial_scores = jnp.sum(by_seq[:, :, None] * member[None, :, :], axis=1)
    return lax.psum(partial_scores, "tensor") * factor


def solution(mesh):
    return jax.shard_map(
        shards,
        mesh=mesh,
        in_specs=(
            P("dp"),
            P("dp"),
            P("dp", "tensor"),
            P("dp", None),
            P("dp", "tensor"),
            P("dp", "tensor"),
            P("dp", "tensor"),
            P("tensor", "dp"),
            P("dp", "tensor"),
            P("dp", "tensor"),
            P("dp", "tensor"),
            P("dp", "tensor"),
            P("dp", "tensor"),
        ),
        out_specs=P("dp", None),
        check_vma=False,
    )
```

profile of v0, /device:TPU:0, one launch (start us, length us, event | category | flops | bytes accessed | tf_op | source)
XLA Modules:
  0.0 789.7 jit_solution(15625570581010409672)
XLA Ops:
  8.7 2.5 multiply_convert_fusion.2
  14.9 3.3 convert_bitcast_fusion
  18.2 5.1 copy.78
  23.4 10.4 %copy.46 = f32[2,256,4,8,128]{1,4,3,2,0:T(8,128)} copy(f32[2,256,4,8,128]{4,3,2,1,0:T(8,128)} %bitcast.112) | data formatting | bytes 16777216 | tf_op jit(solution)/shard_map/convert_element_type | solution.py:47
  33.8 4.4 slice_negate_fusion.1
  39.7 3.5 fusion.7
  43.1 10.5 %fusion.68 = (f32[2,4,8,256]{3,2,1,0:T(8,128)S(1)}, f32[2,4,8,256,256]{3,4,2,1,0:T(8,128)}) fusion(pred[256,256]{0,1:T(8,128)(4,1)S(1)} %iota_compare_fusion, bf16[2,256,4,128,1]{1,3,4,2,0:T(8,128)(2,1)S(1)} %fusion.51, bf16[2,256,4,8,128]{1,4,3,2,0:T(8,128)(2,1)} %fusion.7), kind=kOutput, calls=%fused_computation.100 | convolution fusion | flops 1090519296 | bytes 21626880 | tf_op jit(solution)/shard_map/sub | solution.py:58
  53.6 9.3 %fusion.67 = bf16[2,4,8,256,256]{3,4,2,1,0:T(8,128)(2,1)} fusion(f32[2,4,8,256,256]{3,4,2,1,0:T(8,128)} %get-tuple-element.18, f32[2,4,8,256]{3,2,1,0:T(8,128)S(1)} %get-tuple-element.17), kind=kLoop, calls=%fused_computation.99 | loop fusion | flops 8388608 | bytes 25231360 | tf_op jit(solution)/shard_map/convert_element_type | solution.py:60
  62.9 14.6 %copy.60 = bf16[2,4,8,256,256]{4,2,3,1,0:T(8,128)(2,1)} copy(bf16[2,4,8,256,256]{3,4,2,1,0:T(8,128)(2,1)} %fusion.67) | data formatting | bytes 16777216 | tf_op jit(solution)/shard_map/convert_element_type | solution.py:60
  77.6 6.3 convert_bitcast_fusion.1
  83.9 4.7 copy.53
  88.5 7.6 reshape.190
  96.1 9.7 %multiply_convert_fusion = bf16[512,8192]{1,0:T(8,128)(2,1)} fusion(bf16[512,8192]{1,0:T(8,128)(2,1)} %param.16, f32[512]{0:T(512)S(1)} %compare_convert_fusion.1), kind=kLoop, calls=%fused_computation.8 | loop fusion | flops 12582912 | bytes 16779264 | tf_op jit(solution)/shard_map/convert_element_type | solution.py:103
  105.8 10.2 %fusion.30 = bf16[1,512,1024]{2,1,0:T(8,128)(2,1)} fusion(bf16[512,4096]{1,0:T(8,128)(2,1)} %param.15, bf16[1024,4096]{1,0:T(8,128)(2,1)} %all-gather.11.cloned.1.call-done), kind=kOutput, calls=%fused_computation.44 | convolution fusion | flops 4295491584 | bytes 13631488 | tf_op jit(solution)/shard_map/dot_general | solution.py:34
  116.0 46.5 %all-gather.7.cloned.1.call-done = bf16[1024,4096]{1,0:T(8,128)(2,1)} async-done(((bf16[64,4096]{1,0:T(8,128)(2,1)}), bf16[1024,4096]{1,0:T(8,128)(2,1)}) %all-gather.7.cloned.1.call-update) | async-done | bytes 8388624 | tf_op jit(solution)/shard_map/all_gather | solution.py:140
  162.5 10.2 %fusion.29 = bf16[1,512,1024]{2,1,0:T(8,128)(2,1)} fusion(bf16[512,4096]{1,0:T(8,128)(2,1)} %reshape.190, bf16[1024,4096]{1,0:T(8,128)(2,1)} %all-gather.7.cloned.1.call-done), kind=kOutput, calls=%fused_computation.43 | convolution fusion | flops 4295491584 | bytes 13631488 | tf_op jit(solution)/shard_map/dot_general | solution.py:34
  172.7 65.2 %all-gather.9.cloned.1.call-done = bf16[1024,4096]{1,0:T(8,128)(2,1)} async-done(((bf16[64,4096]{1,0:T(8,128)(2,1)}), bf16[1024,4096]{1,0:T(8,128)(2,1)}) %all-gather.9.cloned.1.call-update) | async-done | bytes 8388624 | tf_op jit(solution)/shard_map/all_gather | solution.py:139
  237.9 10.4 %fusion.31 = bf16[1,512,1024]{2,1,0:T(8,128)(2,1)} fusion(bf16[1024,4096]{1,0:T(8,128)(2,1)} %all-gather.9.cloned.1.call-done, bf16[512,8192]{1,0:T(8,128)(2,1)} %multiply_convert_fusion, s32[]{:T(128)S(6)} %select_n.17), kind=kOutput, calls=%fused_computation.45 | convolution fusion | flops 4295491584 | bytes 13631492 | tf_op jit(solution)/shard_map/dot_general | solution.py:34
  248.2 315.4 %all-gather.13.cloned.1.call-done = bf16[4096,8192]{1,0:T(8,128)(2,1)} async-done(((bf16[4096,512]{1,0:T(8,128)(2,1)}), bf16[4096,8192]{1,0:T(8,128)(2,1)}) %all-gather.13.cloned.1.call-update) | async-done | bytes 67108880 | tf_op jit(solution)/shard_map/all_gather | solution.py:104
  563.6 42.0 %fusion.25 = bf16[64,8,32,128]{3,1,2,0:T(8,128)(2,1)S(1)} fusion(bf16[512,8192]{1,0:T(8,128)(2,1)} %multiply_convert_fusion, bf16[4096,8192]{1,0:T(8,128)(2,1)} %all-gather.13.cloned.1.call-done), kind=kOutput, calls=%fused_computation.38 | convolution fusion | flops 34361835520 | bytes 79691776 | tf_op jit(solution)/shard_map/dot_general | solution.py:34
  608.9 8.2 %fusion.18 = f32[2,4,256,8,256]{2,4,3,1,0:T(8,128)} fusion(bf16[2,256,4,8,128]{4,3,2,1,0:T(8,128)(2,1)S(1)} %bitcast.113, bf16[2,256,4,128,1]{3,2,1,0,4:T(4,128)(2,1)S(1)} %bitcast.116), kind=kOutput, calls=%fused_computation.31 | convolution fusion | flops 1073741824 | bytes 21495808 | tf_op jit(solution)/shard_map/slkgd,smkd->skglm/dot_general | solution.py:64
  617.2 27.2 %fusion.22 = f32[2,256,4,8,128]{1,4,3,2,0:T(8,128)} fusion(bf16[2,256,4,128,1]{1,3,4,2,0:T(8,128)(2,1)S(1)} %fusion.51, f32[2,4,256,8,256]{2,4,3,1,0:T(8,128)} %fusion.18, f32[2,4,8,256,256]{3,4,2,1,0:T(8,128)} %get-tuple-element.18, f32[2,4,8,256]{3,2,1,0:T(8,128)S(1)} %get-tuple-element.17), kind=kOutput, calls=%fused_computation.36 | convolution fusion | flops 1103118592 | bytes 42532864 | tf_op jit(solution)/shard_map/skglm,smkd->slkgd/dot_general | solution.py:69
  644.4 4.4 slice_negate_fusion
  650.4 3.7 fusion.9
  654.1 7.9 %copy.57 = bf16[2,256,4,8,128]{4,3,2,1,0:T(8,128)(2,1)} copy(bf16[2,256,4,8,128]{1,4,3,2,0:T(8,128)(2,1)} %fusion.9) | data formatting | bytes 8388608 | tf_op jit(solution)/shard_map/convert_element_type | solution.py:78
  662.0 7.4 reshape.192
  669.4 25.6 %fusion.38 = f32[2,256,4,128]{1,3,2,0:T(8,128)S(1)} fusion(bf16[2,256,4,8,128]{1,4,3,2,0:T(8,128)(2,1)} %fusion.7, f32[2,4,256,8,256]{2,4,3,1,0:T(8,128)} %fusion.18, f32[2,4,8,256,256]{3,4,2,1,0:T(8,128)} %get-tuple-element.18, f32[2,4,8,256]{3,2,1,0:T(8,128)S(1)} %get-tuple-element.17), kind=kOutput, calls=%fused_computation.48 | convolution fusion | flops 1103118592 | bytes 38862848 | tf_op jit(solution)/shard_map/skglm,slkgd->smkd/dot_general | solution.py:72
  695.3 6.3 fusion.42
  703.5 10.5 %fusion.69 = f32[512,1024]{1,0:T(8,128)} fusion(bf16[512,4096]{1,0:T(8,128)(2,1)} %reshape.192, bf16[1024,4096]{1,0:T(8,128)(2,1)} %all-gather.15.cloned.1.call-done), kind=kOutput, calls=%fused_computation.101 | convolution fusion | flops 4294967296 | bytes 14680064 | tf_op jit(solution)/shard_map/dot_general | solution.py:34
  714.0 3.7 fusion.34
  720.0 54.1 %reduce-scatter.2.cloned.1.call-done = bf16[4,512,512]{2,1,0:T(8,128)(2,1)} async-done(((bf16[4,512,1024]{2,1,0:T(8,128)(2,1)}), bf16[4,512,512]{2,1,0:T(8,128)(2,1)}) %reduce-scatter.2.cloned.1.call-update) | async-done | bytes 2097168 | tf_op jit(solution)/shard_map/reduce_scatter | solution.py:146
  777.0 4.9 psum.7
  (72 shorter events, 19.7 us)
Async XLA Ops:
  6.5 6.0 copy-start.12
  6.5 6.9 copy-start.10
  6.5 8.2 %copy-start.13 = (s32[512]{0:T(512)S(1)}, s32[512]{0:T(512)}, u32[]{:S(2)}) copy-start(s32[512]{0:T(512)} %param.13) | copy-start | bytes 6148
  6.5 8.3 %copy-start.11 = (bf16[512,512]{1,0:T(8,128)(2,1)S(1)}, bf16[512,512]{1,0:T(8,128)(2,1)}, u32[]{:S(2)}) copy-start(bf16[512,512]{1,0:T(8,128)(2,1)} %param.19) | copy-start | bytes 1572868
  6.5 99.3 %all-gather.11.cloned.1.call-start = ((), (), s32[]{:S(2)}) async-start(), calls=%async_computation.3 | async-start | bytes 8912896 | tf_op jit(solution)/shard_map/all_gather | solution.py:138
  7.3 155.2 %all-gather.7.cloned.1.call-start = ((), (), s32[]{:S(2)}) async-start(), calls=%async_computation.1 | async-start | bytes 8912896 | tf_op jit(solution)/shard_map/all_gather | solution.py:140
  8.0 229.8 %all-gather.9.cloned.1.call-start = ((), (), s32[]{:S(2)}) async-start(), calls=%async_computation.2 | async-start | bytes 8912896 | tf_op jit(solution)/shard_map/all_gather | solution.py:139
  11.3 552.4 %all-gather.13.cloned.1.call-start = ((), (), s32[]{:S(2)}) async-start(), calls=%async_computation.4 | async-start | bytes 71303168 | tf_op jit(solution)/shard_map/all_gather | solution.py:104
  11.9 691.6 %all-gather.15.cloned.1.call-start = ((), (), s32[]{:S(2)}) async-start(), calls=%async_computation.5 | async-start | bytes 8912896 | tf_op jit(solution)/shard_map/all_gather | solution.py:141
  12.5 701.5 %all-gather.17.cloned.1.call-start = ((), (), s32[]{:S(2)}) async-start(), calls=%async_computation.6 | async-start | bytes 2228224 | tf_op jit(solution)/shard_map/all_gather | solution.py:142
  13.3 760.8 %reduce-scatter.2.cloned.1.call-start = ((), (), s32[]{:S(2)}) async-start(), calls=%async_computation.7 | async-start | bytes 6291456 | tf_op jit(solution)/shard_map/reduce_scatter | solution.py:146
  14.8 23.7 %copy-start.3 = (f32[256,128]{0,1:T(8,128)}, f32[256,128]{0,1:T(8,128)S(1)}, u32[]{:S(2)}) copy-start(f32[256,128]{0,1:T(8,128)S(1)} %get-tuple-element.13) | copy-start | bytes 393220
  14.8 23.7 %copy-start.5 = (f32[256,128]{0,1:T(8,128)}, f32[256,128]{0,1:T(8,128)S(1)}, u32[]{:S(2)}) copy-start(f32[256,128]{0,1:T(8,128)S(1)} %get-tuple-element.14) | copy-start | bytes 393220
  33.8 5.9 copy-start
  606.9 2.0 copy-start.2
  644.4 6.0 copy-start.1
  644.4 6.0 copy-start.4
  644.4 6.0 copy-start.6
  714.0 3.7 copy-start.7
  714.0 3.7 copy-start.8
  714.0 3.7 copy-start.9
Sparse Core Ops, SparseCore 0:
  9.5 77.5 all-gather.10
  89.3 73.1 all-gather.6
  164.7 73.1 all-gather.8
  239.3 324.3 all-gather.12
  565.7 74.8 all-gather.14
  642.6 39.6 all-gather.16
  720.1 53.9 reduce-scatter.1
where the time goes:
time: 795 us; the launch traced here: 790 us
  waiting for transfers between devices  484 us (61%)
  matrix products  171 us (22%)
  local copies, waits for them, and re-layouts  66.3 us (8%)
  other arithmetic  49.2 us (6%)
  between operations  14.3 us (2%)
    all_gather x1, waiting for transfers between devices, shards(): lax.all_gather(out_weight, 'dp', axis=1, tiled=True)  315 us
    dot_general x6, matrix products, outer_rows(): lax.dot_general(left, right, (((1,), (1,)), ((), ())), preferred_element_...  87 us
    all_gather x1, waiting for transfers between devices, shards(): lax.all_gather(val_dy, 'dp', axis=0, tiled=True)  65.2 us
    reduce_scatter x1, waiting for transfers between devices, shards(): lax.psum_scatter(gram_parts.astype(jnp.bfloat16), 'tensor', scatter_dimen...  54.1 us
    all_gather x1, waiting for transfers between devices, shards(): lax.all_gather(val_attention, 'dp', axis=0, tiled=True)  46.5 us
    dot_general x1, matrix products, sequence_pass(): jnp.einsum('skglm,smkd->slkgd', logit_grad, key_rot, preferred_element_ty...  27.2 us
    dot_general x1, matrix products, sequence_pass(): jnp.einsum('skglm,slkgd->smkd', logit_grad, query_rot, preferred_element_...  25.6 us
  transfers between devices with their start and end apart: 7, of which 4 were waited for; matrix products, arithmetic and copies ran while one was open for 35% of the time, Pallas kernels for 0%

commit v1 on v0

--- a/solution.py
+++ b/solution.py
@@ -36,7 +36,7 @@
     )
 
 
-def sequence_pass(query_raw, key_raw, value_part, grad_out):
+def attend(query_raw, key_raw, value_part):
     seq_len, head_width = (key_raw.shape[1], key_raw.shape[-1])
     cos_table, sine_table = rotation(seq_len, head_width)
     score_scale = 1.0 / math.sqrt(head_width)
@@ -61,6 +61,18 @@
     attended = jnp.einsum(
         "skglm,smkd->slkgd", probs_low, value_part, preferred_element_type=jnp.float32
     ).astype(jnp.bfloat16)
+    return attended, (query_rot, key_rot, attn_probs, probs_low)
+
+
+def attend_back(saved, value_part, grad_out):
+    query_rot, key_rot, attn_probs, probs_low = saved
+    seq_len, head_width = (key_rot.shape[1], key_rot.shape[-1])
+    cos_table, sine_table = rotation(seq_len, head_width)
+    score_scale = 1.0 / math.sqrt(head_width)
+    q_cos = cos_table[None, :, None, None, :]
+    q_sine = sine_table[None, :, None, None, :]
+    k_cos = cos_table[None, :, None, :]
+    k_sine = sine_table[None, :, None, :]
     prob_grad = jnp.einsum(
         "slkgd,smkd->skglm", grad_out, value_part, preferred_element_type=jnp.float32
     )
@@ -77,7 +89,19 @@
     )
     dquery_raw = (dquery * q_cos - turn_half(dquery) * q_sine).astype(jnp.bfloat16)
     dkey_raw = (key_grad * k_cos - turn_half(key_grad) * k_sine).astype(jnp.bfloat16)
-    return (attended, dquery_raw, jnp.stack([dkey_raw, dvalue.astype(jnp.bfloat16)], axis=3))
+    return dquery_raw, jnp.stack([dkey_raw, dvalue.astype(jnp.bfloat16)], axis=3)
+
+
+def exchange(parts, count):
+    width = parts.shape[2] // count
+    me = lax.axis_index("tensor")
+    total = lax.dynamic_slice_in_dim(parts, me * width, width, 2).astype(jnp.float32)
+    for step in range(1, count):
+        target = lax.rem(me + step, count)
+        sent = lax.dynamic_slice_in_dim(parts, target * width, width, 2)
+        pairs = [(src, (src + step) % count) for src in range(count)]
+        total = total + lax.ppermute(sent, "tensor", pairs).astype(jnp.float32)
+    return total
 
 
 def shards(
@@ -100,53 +124,49 @@
     kv_local = key_rows.shape[1] // HD
     head_group = HEADS // KV
     live_rows = (cand_ids != pad_token).astype(jnp.float32)[:, None]
+    val_live = (val_ids != pad_token).astype(jnp.float32)[:, None]
+
+    def val_masked(rows):
+        return (rows.astype(jnp.float32) * val_live).astype(jnp.bfloat16)
+
+    weight = lax.all_gather(out_weight, "dp", axis=1, tiled=True)
+    early_rows = jnp.concatenate([val_attention, val_masked(val_cotangents), val_inputs], axis=1)
+    late_rows = jnp.concatenate(
+        [val_masked(val_query_grads), val_masked(val_keyvalue_grads)], axis=1
+    )
     masked = (cotangent.astype(jnp.float32) * live_rows).astype(jnp.bfloat16)
-    grad_attn = outer_rows(masked, lax.all_gather(out_weight, "dp", axis=1, tiled=True)).astype(
-        jnp.bfloat16
-    )
     q_shape = (seq_count, LEN, kv_local, head_group, HD)
     kv_shape = (seq_count, LEN, kv_local, HD)
-    attended, dquery, kv_grads = sequence_pass(
-        queries.reshape(q_shape),
-        key_rows.reshape(kv_shape),
-        value_rows.reshape(kv_shape),
-        grad_attn.reshape(q_shape),
+    value_part = value_rows.reshape(kv_shape)
+    attended, saved = attend(queries.reshape(q_shape), key_rows.reshape(kv_shape), value_part)
+    attended = attended.reshape(tok_rows, -1)
+    weight, early_rows, late_rows, attended, masked = lax.optimization_barrier(
+        (weight, early_rows, late_rows, attended, masked)
     )
-    attended = attended.reshape(tok_rows, -1)
+    early = lax.all_gather(early_rows, "dp", axis=0, tiled=True)
+    late = lax.all_gather(late_rows, "dp", axis=0, tiled=True)
+    grad_attn = outer_rows(masked, weight).astype(jnp.bfloat16)
+    dquery, kv_grads = attend_back(saved, value_part, grad_attn.reshape(q_shape))
     dquery = dquery.reshape(tok_rows, -1)
     kv_grads = kv_grads.reshape(tok_rows, -1)
+    early, dquery, kv_grads = lax.optimization_barrier((early, dquery, kv_grads))
     feat_block = val_cotangents.shape[1]
     own_cotangent = lax.dynamic_slice_in_dim(
         masked, lax.axis_index("tensor") * feat_block, feat_block, 1
     )
-    val_live = (val_ids != pad_token).astype(jnp.float32)[:, None]
-    val_dy = (val_cotangents.astype(jnp.float32) * val_live).astype(jnp.bfloat16)
-    val_dq = (val_query_grads.astype(jnp.float32) * val_live).astype(jnp.bfloat16)
-    val_dkv = (val_keyvalue_grads.astype(jnp.float32) * val_live).astype(jnp.bfloat16)
-
-    def gram_stack(part_x, part_dy, part_attn, part_dq, part_dkv):
-        return jnp.stack(
-            [
-                outer_rows(attended, part_attn),
-                outer_rows(own_cotangent, part_dy),
-                outer_rows(inputs, part_x),
-                outer_rows(dquery, part_dq) + outer_rows(kv_grads, part_dkv),
-            ]
-        )
-
-    gathered = (
-        lax.all_gather(val_inputs, "dp", axis=0, tiled=True),
-        lax.all_gather(val_dy, "dp", axis=0, tiled=True),
-        lax.all_gather(val_attention, "dp", axis=0, tiled=True),
-        lax.all_gather(val_dq, "dp", axis=0, tiled=True),
-        lax.all_gather(val_dkv, "dp", axis=0, tiled=True),
+    n_tensor = lax.axis_size("tensor")
+    gram_attn = outer_rows(attended, early[:, :feat_block])
+    gram_cot = outer_rows(own_cotangent, early[:, feat_block : 2 * feat_block])
+    gram_input = outer_rows(inputs, early[:, 2 * feat_block :])
+    early_share = exchange(
+        jnp.stack([gram_attn, gram_cot, gram_input]).astype(jnp.bfloat16), n_tensor
     )
-    gram_parts = gram_stack(*gathered)
+    gram_proj = outer_rows(dquery, late[:, :feat_block]) + outer_rows(
+        kv_grads, late[:, feat_block:]
+    )
+    late_share = exchange(gram_proj[None].astype(jnp.bfloat16), n_tensor)
     factor = 1.0 / (64.0 * D)
-    gram_share = lax.psum_scatter(
-        gram_parts.astype(jnp.bfloat16), "tensor", scatter_dimension=2, tiled=True
-    ).astype(jnp.float32)
-    product = gram_share[0] * gram_share[1] + gram_share[2] * gram_share[3]
+    product = early_share[0] * early_share[1] + early_share[2] * late_share[0]
     col_width = product.shape[1]
     by_seq = jnp.sum(product.reshape(seq_count, LEN, col_width), axis=1)
     column = lax.axis_index("tensor") * col_width + jnp.arange(col_width)

time: 795 us -> 604 us (0.76)
  waiting for transfers between devices: 484 us -> 292 us
  matrix products: 171 us -> 162 us
  local copies, waits for them, and re-layouts: 66.3 us -> 75.1 us
    all_gather x6 -> x3, waiting for transfers between devices: 427 us -> 280 us  [the longest x1 246 us: shards(): weight = lax.all_gather(out_weight, 'dp', axis=1, tiled=True)]
    reduce_scatter x1 -> x0, waiting for transfers between devices: 54.1 us -> none  [shards(): lax.psum_scatter(gram_parts.astype(jnp.bfloat16), 'tensor', scatter_dimen...]
    ppermute x0 -> x2, waiting for transfers between devices: none -> 10.6 us  [exchange(): total = total + lax.ppermute(sent, 'tensor', pairs).astype(jnp.float32)]
    dot_general x6, matrix products: 87 us -> 77.3 us  [outer_rows(): lax.dot_general(left, right, (((1,), (1,)), ((), ())), preferred_element_...]
    convert_element_type x7 -> x6, other arithmetic: 22.2 us -> 14.5 us  [the longest x1 7.13 us: attend(): probs_low = attn_probs.astype(jnp.bfloat16)]
  transfers between devices with their start and end apart: 7 -> 5, of which waited for: 4 -> 3; matrix products, arithmetic and copies ran while one was open for 35% -> 46% of each run, Pallas kernels for 0% -> 0%
where the time goes in v1:
time: 604 us; the launch traced here: 596 us
  waiting for transfers between devices  292 us (48%)
  matrix products  162 us (27%)
  local copies, waits for them, and re-layouts  75.1 us (12%)
  other arithmetic  45 us (7%)
  between operations  13.7 us (2%)
    all_gather x1, waiting for transfers between devices, shards(): weight = lax.all_gather(out_weight, 'dp', axis=1, tiled=True)  246 us
    dot_general x6, matrix products, outer_rows(): lax.dot_general(left, right, (((1,), (1,)), ((), ())), preferred_element_...  77.3 us
    all_gather x1, waiting for transfers between devices, shards(): late = lax.all_gather(late_rows, 'dp', axis=0, tiled=True)  33.7 us
    dot_general x1, matrix products, attend_back(): jnp.einsum('skglm,smkd->slkgd', logit_grad, key_rot, preferred_element_ty...  27.6 us
    dot_general x1, matrix products, attend_back(): jnp.einsum('skglm,slkgd->smkd', logit_grad, query_rot, preferred_element_...  26.7 us
    convert_element_type x1, local copies, waits for them, and re-layouts, attend(): probs_low = attn_probs.astype(jnp.bfloat16)  15.2 us
    unnamed x40, local copies, waits for them, and re-layouts  15.1 us
  transfers between devices with their start and end apart: 5, of which 3 were waited for; matrix products, arithmetic and copies ran while one was open for 46% of the time, Pallas kernels for 0%

profile of v1, /device:TPU:0, one launch (start us, length us, event | category | flops | bytes accessed | tf_op | source)
XLA Modules:
  0.0 595.9 jit_solution(2933177354365329173)
XLA Ops:
  7.3 3.3 convert_bitcast_fusion
  10.6 5.1 copy.78
  15.7 10.3 %copy.46 = f32[2,256,4,8,128]{1,4,3,2,0:T(8,128)} copy(f32[2,256,4,8,128]{4,3,2,1,0:T(8,128)} %bitcast.114) | data formatting | bytes 16777216 | tf_op jit(solution)/shard_map/convert_element_type | solution.py:47
  27.8 4.6 slice_negate_fusion.1
  34.1 3.4 fusion.9
  37.5 10.5 %fusion.92 = (f32[2,4,8,256]{3,2,1,0:T(8,128)S(1)}, f32[2,4,8,256,256]{3,4,2,1,0:T(8,128)}) fusion(pred[256,256]{0,1:T(8,128)(4,1)S(1)} %iota_compare_fusion, bf16[2,256,4,128,1]{1,3,4,2,0:T(8,128)(2,1)S(1)} %fusion.75, bf16[2,256,4,8,128]{1,4,3,2,0:T(8,128)(2,1)} %fusion.9), kind=kOutput, calls=%fused_computation.114 | convolution fusion | flops 1090519296 | bytes 21626880 | tf_op jit(solution)/shard_map/sub | solution.py:58
  48.0 7.1 %fusion.91 = bf16[2,4,8,256,256]{3,4,2,1,0:T(8,128)(2,1)S(1)} fusion(f32[2,4,8,256,256]{3,4,2,1,0:T(8,128)} %get-tuple-element.34, f32[2,4,8,256]{3,2,1,0:T(8,128)S(1)} %get-tuple-element.33), kind=kLoop, calls=%fused_computation.113 | loop fusion | flops 8388608 | bytes 25231360 | tf_op jit(solution)/shard_map/convert_element_type | solution.py:60
  55.2 3.2 copy-done
  58.4 5.0 convert_bitcast_fusion.1
  63.4 7.1 %copy.53 = bf16[2,256,4,8,128]{4,3,2,1,0:T(8,128)(2,1)} copy(bf16[2,256,4,8,128]{4,1,3,2,0:T(8,128)(2,1)} %convert_bitcast_fusion.1) | data formatting | bytes 8388608 | tf_op jit(solution)/shard_map/convert_element_type | solution.py:63
  70.5 7.3 %reshape.195 = bf16[512,4096]{1,0:T(8,128)(2,1)} reshape(bf16[2,256,4,8,128]{4,3,2,1,0:T(8,128)(2,1)} %copy.53) | data formatting | bytes 8388608 | tf_op jit(solution)/shard_map/reshape | solution.py:142
  79.2 2.3 pad_maximum_fusion.1
  81.5 9.8 %multiply_convert_fusion = bf16[512,8192]{1,0:T(8,128)(2,1)} fusion(bf16[512,8192]{1,0:T(8,128)(2,1)} %param.16, f32[512]{0:T(512)S(1)} %compare_convert_fusion), kind=kLoop, calls=%fused_computation.8 | loop fusion | flops 12582912 | bytes 16779264 | tf_op jit(solution)/shard_map/convert_element_type | solution.py:137
  91.3 246.4 %all-gather.4.cloned.1.call-done = bf16[4096,8192]{1,0:T(8,128)(2,1)} async-done(((bf16[4096,512]{1,0:T(8,128)(2,1)}), bf16[4096,8192]{1,0:T(8,128)(2,1)}) %all-gather.4.cloned.1.call-update) | async-done | bytes 67108880 | tf_op jit(solution)/shard_map/all_gather | solution.py:132
  338.5 15.2 %copy.60 = bf16[2,4,8,256,256]{4,2,3,1,0:T(8,128)(2,1)} copy(bf16[2,4,8,256,256]{3,4,2,1,0:T(8,128)(2,1)} %copy-done) | data formatting | bytes 16777216 | tf_op jit(solution)/shard_map/convert_element_type | solution.py:60
  354.3 42.3 %fusion.32 = bf16[64,8,32,128]{3,1,2,0:T(8,128)(2,1)S(1)} fusion(bf16[512,8192]{1,0:T(8,128)(2,1)} %multiply_convert_fusion, bf16[4096,8192]{1,0:T(8,128)(2,1)} %all-gather.4.cloned.1.call-done), kind=kOutput, calls=%fused_computation.46 | convolution fusion | flops 34361835520 | bytes 79691776 | tf_op jit(solution)/shard_map/dot_general | solution.py:34
  400.0 8.5 %fusion.26 = f32[2,4,256,8,256]{2,4,3,1,0:T(8,128)} fusion(bf16[2,256,4,8,128]{4,3,2,1,0:T(8,128)(2,1)S(1)} %bitcast.115, bf16[2,256,4,128,1]{3,2,1,0,4:T(4,128)(2,1)S(1)} %bitcast.118), kind=kOutput, calls=%fused_computation.38 | convolution fusion | flops 1073741824 | bytes 21495808 | tf_op jit(solution)/shard_map/slkgd,smkd->skglm/dot_general | solution.py:76
  408.5 26.7 %fusion.57 = f32[2,256,4,128]{1,3,2,0:T(8,128)S(1)} fusion(bf16[2,256,4,8,128]{1,4,3,2,0:T(8,128)(2,1)} %fusion.9, f32[2,4,256,8,256]{2,4,3,1,0:T(8,128)} %fusion.26, f32[2,4,8,256,256]{3,4,2,1,0:T(8,128)} %get-tuple-element.34, f32[2,4,8,256]{3,2,1,0:T(8,128)S(1)} %get-tuple-element.33), kind=kOutput, calls=%fused_computation.57 | convolution fusion | flops 1103118592 | bytes 38862848 | tf_op jit(solution)/shard_map/skglm,slkgd->smkd/dot_general | solution.py:84
  435.5 6.6 %fusion.66 = bf16[2,256,4,1,128]{1,4,2,0,3:T(8,128)(2,1)S(1)} fusion(bf16[2,4,8,256,256]{4,2,3,1,0:T(8,128)(2,1)} %copy.60, bf16[2,256,4,8,128]{4,3,2,1,0:T(8,128)(2,1)} %bitcast.116), kind=kOutput, calls=%fused_computation.60 | convolution fusion | flops 1074003968 | bytes 13107200 | tf_op jit(solution)/shard_map/skglm,slkgd->smkd/dot_general | solution.py:87
  444.8 27.6 %fusion.29 = f32[2,256,4,8,128]{1,4,3,2,0:T(8,128)} fusion(bf16[2,256,4,128,1]{1,3,4,2,0:T(8,128)(2,1)S(1)} %copy-done.11, f32[2,4,256,8,256]{2,4,3,1,0:T(8,128)} %fusion.26, f32[2,4,8,256,256]{3,4,2,1,0:T(8,128)} %get-tuple-element.34, f32[2,4,8,256]{3,2,1,0:T(8,128)S(1)} %get-tuple-element.33), kind=kOutput, calls=%fused_computation.42 | convolution fusion | flops 1103118592 | bytes 42532864 | tf_op jit(solution)/shard_map/skglm,smkd->slkgd/dot_general | solution.py:81
  472.4 4.4 slice_negate_fusion
  478.5 3.4 fusion.11
  481.9 8.0 %copy.57 = bf16[2,256,4,8,128]{4,3,2,1,0:T(8,128)(2,1)} copy(bf16[2,256,4,8,128]{1,4,3,2,0:T(8,128)(2,1)} %fusion.11) | data formatting | bytes 8388608 | tf_op jit(solution)/shard_map/convert_element_type | solution.py:90
  489.8 7.3 %reshape.197 = bf16[512,4096]{1,0:T(8,128)(2,1)} reshape(bf16[2,256,4,8,128]{4,3,2,1,0:T(8,128)(2,1)} %copy.57) | data formatting | bytes 8388608 | tf_op jit(solution)/shard_map/reshape | solution.py:150
  497.1 9.3 %fusion.58 = bf16[1,512,1024]{2,1,0:T(8,128)(2,1)S(1)} fusion(bf16[1024,12288]{1,0:T(8,128)(2,1)} %all-gather.6.cloned.1.call-done, bf16[512,8192]{1,0:T(8,128)(2,1)} %multiply_convert_fusion, s32[]{:T(128)S(6)} %select_n.25), kind=kOutput, calls=%fused_computation.58 | convolution fusion | flops 4295491584 | bytes 13631492 | tf_op jit(solution)/shard_map/dot_general | solution.py:34
  506.5 7.7 %fusion.51 = bf16[1,512,1024]{2,1,0:T(8,128)(2,1)S(1)} fusion(bf16[512,4096]{1,0:T(8,128)(2,1)S(1)} %copy-done.15, bf16[1024,12288]{1,0:T(8,128)(2,1)} %all-gather.6.cloned.1.call-done), kind=kOutput, calls=%fused_computation.55 | convolution fusion | flops 4295491584 | bytes 13631488 | tf_op jit(solution)/shard_map/dot_general | solution.py:34
  514.2 7.3 %fusion.48 = bf16[1,512,1024]{2,1,0:T(8,128)(2,1)S(1)} fusion(bf16[512,4096]{1,0:T(8,128)(2,1)S(1)} %copy-done.3, bf16[1024,12288]{1,0:T(8,128)(2,1)} %all-gather.6.cloned.1.call-done), kind=kOutput, calls=%fused_computation.54 | convolution fusion | flops 4295491584 | bytes 13631488 | tf_op jit(solution)/shard_map/dot_general | solution.py:34
  524.5 33.7 %all-gather.8.cloned.1.call-done = bf16[1024,5120]{1,0:T(8,128)(2,1)} async-done(((bf16[64,5120]{1,0:T(8,128)(2,1)}), bf16[1024,5120]{1,0:T(8,128)(2,1)}) %all-gather.8.cloned.1.call-update) | async-done | bytes 10485776 | tf_op jit(solution)/shard_map/all_gather | solution.py:147
  558.2 3.3 fusion.33
  561.5 7.3 %add_convert_fusion = bf16[512,1024]{1,0:T(8,128)(2,1)S(1)} fusion(f32[512,1024]{1,0:T(8,128)S(1)} %fusion.33, bf16[512,4096]{1,0:T(8,128)(2,1)S(1)} %copy-done.4, bf16[1024,5120]{1,0:T(8,128)(2,1)} %all-gather.8.cloned.1.call-done), kind=kOutput, calls=%fused_computation.49 | convolution fusion | flops 4296015872 | bytes 15728640 | tf_op jit(solution)/shard_map/dot_general | solution.py:34
  572.4 10.6 %collective-permute-done.1 = bf16[1,512,512]{2,1,0:T(8,128)(2,1)S(1)} collective-permute-done((bf16[1,512,512]{2,1,0:T(8,128)(2,1)S(1)}, bf16[1,512,512]{2,1,0:T(8,128)(2,1)S(1)}, u32[]{:S(2)}, u32[]{:S(2)}) %collective-permute-start.1) | collective-permute-done | bytes 524320 | tf_op jit(solution)/shard_map/ppermute | solution.py:103
  583.7 4.9 psum.7
  (79 shorter events, 22.4 us)
Async XLA Ops:
  6.5 331.2 %all-gather.4.cloned.1.call-start = ((), (), s32[]{:S(2)}) async-start(), calls=%async_computation | async-start | bytes 71303168 | tf_op jit(solution)/shard_map/all_gather | solution.py:132
  7.3 489.9 %all-gather.6.cloned.1.call-start = ((), (), s32[]{:S(2)}) async-start(), calls=%async_computation.1 | async-start | bytes 26738688 | tf_op jit(solution)/shard_map/all_gather | solution.py:146
  15.7 10.3 %copy-start.5 = (bf16[512,512]{1,0:T(8,128)(2,1)S(1)}, bf16[512,512]{1,0:T(8,128)(2,1)}, u32[]{:S(2)}) copy-start(bf16[512,512]{1,0:T(8,128)(2,1)} %param.18) | copy-start | bytes 1572868
  15.7 11.0 %copy-start.8 = (bf16[512,512]{1,0:T(8,128)(2,1)S(1)}, bf16[512,512]{1,0:T(8,128)(2,1)}, u32[]{:S(2)}) copy-start(bf16[512,512]{1,0:T(8,128)(2,1)} %param.19) | copy-start | bytes 1572868
  27.6 4.8 slice-start
  27.8 9.7 %copy-start.10 = (bf16[2,256,4,128,1]{1,3,4,2,0:T(8,128)(2,1)}, bf16[2,256,4,128,1]{1,3,4,2,0:T(8,128)(2,1)S(1)}, u32[]{:S(2)}) copy-start(bf16[2,256,4,128,1]{1,3,4,2,0:T(8,128)(2,1)S(1)} %fusion.75) | copy-start | bytes 1572868
  27.8 6.3 %slice-start.1 = ((s8[8388608]{0:T(1024)(128)(4,1)}), s8[4194304]{0:T(1024)(128)(4,1)S(1)}, s32[]{:S(2)}) async-start(s8[8388608]{0:T(1024)(128)(4,1)} %bitcast.112), calls=%async_computation.4 | async-start | bytes 8388608
  55.2 3.2 copy-start
  63.4 14.5 %copy-start.16 = (s32[64]{0:T(128)S(1)}, s32[64]{0:T(128)}, u32[]{:S(2)}) copy-start(s32[64]{0:T(128)} %param.14) | copy-start | bytes 772
  63.4 14.5 %copy-start.14 = (s32[512]{0:T(512)S(1)}, s32[512]{0:T(512)}, u32[]{:S(2)}) copy-start(s32[512]{0:T(512)} %param.13) | copy-start | bytes 6148
  63.4 14.5 %copy-start.12 = (bf16[64,1024]{1,0:T(8,128)(2,1)S(1)}, bf16[64,1024]{1,0:T(8,128)(2,1)}, u32[]{:S(2)}) copy-start(bf16[64,1024]{1,0:T(8,128)(2,1)} %param.25) | copy-start | bytes 393220
  63.4 14.6 %copy-start.6 = (bf16[64,4096]{1,0:T(8,128)(2,1)S(1)}, bf16[64,4096]{1,0:T(8,128)(2,1)}, u32[]{:S(2)}) copy-start(bf16[64,4096]{1,0:T(8,128)(2,1)} %param.24) | copy-start | bytes 1572868
  63.4 14.6 %copy-start.7 = (bf16[64,4096]{1,0:T(8,128)(2,1)S(1)}, bf16[64,4096]{1,0:T(8,128)(2,1)}, u32[]{:S(2)}) copy-start(bf16[64,4096]{1,0:T(8,128)(2,1)} %param.22) | copy-start | bytes 1572868
  63.4 15.7 %copy-start.9 = (bf16[64,4096]{1,0:T(8,128)(2,1)S(1)}, bf16[64,4096]{1,0:T(8,128)(2,1)}, u32[]{:S(2)}) copy-start(bf16[64,4096]{1,0:T(8,128)(2,1)} %param.21) | copy-start | bytes 1572868
  337.8 220.4 %all-gather.8.cloned.1.call-start = ((), (), s32[]{:S(2)}) async-start(), calls=%async_computation.2 | async-start | bytes 11141120 | tf_op jit(solution)/shard_map/all_gather | solution.py:147
  397.9 2.1 copy-start.2
  435.5 9.2 %copy-start.11 = (bf16[2,256,4,128,1]{1,3,4,2,0:T(8,128)(2,1)S(1)}, bf16[2,256,4,128,1]{1,3,4,2,0:T(8,128)(2,1)}, u32[]{:S(2)}) copy-start(bf16[2,256,4,128,1]{1,3,4,2,0:T(8,128)(2,1)} %copy-done.10) | copy-start | bytes 1572868
  472.4 6.1 %copy-start.1 = (f32[2,256,4,8,128]{1,4,3,2,0:T(8,128)S(1)}, f32[2,256,4,8,128]{1,4,3,2,0:T(8,128)}, u32[]{:S(2)}) copy-start(f32[2,256,4,8,128]{1,4,3,2,0:T(8,128)} %fusion.29) | copy-start | bytes 25165828
  497.1 9.3 %copy-start.15 = (bf16[512,4096]{1,0:T(8,128)(2,1)S(1)}, bf16[512,4096]{1,0:T(8,128)(2,1)}, u32[]{:S(2)}) copy-start(bf16[512,4096]{1,0:T(8,128)(2,1)} %param.15) | copy-start | bytes 12582916
  506.5 7.7 %copy-start.3 = (bf16[512,4096]{1,0:T(8,128)(2,1)S(1)}, bf16[512,4096]{1,0:T(8,128)(2,1)}, u32[]{:S(2)}) copy-start(bf16[512,4096]{1,0:T(8,128)(2,1)} %reshape.195) | copy-start | bytes 12582916
  523.3 47.1 %collective-permute-start = (bf16[3,512,512]{2,1,0:T(8,128)(2,1)}, bf16[3,512,512]{2,1,0:T(8,128)(2,1)}, u32[]{:S(2)}, u32[]{:S(2)}) collective-permute-start(bf16[3,512,512]{2,1,0:T(8,128)(2,1)} %constant_dynamic-slice_fusion), channel_id=1, source_target_pairs={{0,1},{1,0},{2,3},{3,2},{4,5},{5,4},{6,7},{7,6},{8,9},{9,8},{10,11... | collective-permute-start | bytes 4718600 | tf_op jit(solution)/shard_map/ppermute | solution.py:103
  558.2 3.3 copy-start.4
  561.5 8.9 %copy-start.13 = (s32[512]{0:T(512)S(1)}, s32[512]{0:T(512)}, u32[]{:S(2)}) copy-start(s32[512]{0:T(512)} %add_select_fusion) | copy-start | bytes 6148
  568.9 14.2 %collective-permute-start.1 = (bf16[1,512,512]{2,1,0:T(8,128)(2,1)S(1)}, bf16[1,512,512]{2,1,0:T(8,128)(2,1)S(1)}, u32[]{:S(2)}, u32[]{:S(2)}) collective-permute-start(bf16[1,512,512]{2,1,0:T(8,128)(2,1)S(1)} %dynamic-slice_bitcast_fusion), channel_id=1, source_target_pairs={{0,1},{1,0},{2,3},{3,2},{4,5},{5,4},{6,7},{7,6},{8,9},{9,8},{10,11... | collective-permute-start | bytes 1572872 | tf_op jit(solution)/shard_map/ppermute | solution.py:103
Sparse Core Ops, SparseCore 0:
  8.9 328.7 all-gather.3
  339.3 128.5 all-gather.5
  470.2 87.8 all-gather.7

commit v2 on v1

v2 whole, which is shorter than its diff:
```python
import functools
import math

import jax
import jax.numpy as jnp
from jax import lax
from jax.experimental import pallas as pl
from jax.experimental.pallas import tpu as pltpu
from jax.sharding import PartitionSpec as P

D = 8192
HEADS = 64
KV = 8
HD = 128
LEN = 256
VALS = 4


pad_token = 128001
rope_base = 500000.0


def rotation(seq_len, head_width):
    half_dim = head_width // 2
    inv_freq = rope_base ** (-(jnp.arange(half_dim).astype(jnp.float32) * 2.0 / head_width))
    angles = jnp.arange(seq_len).astype(jnp.float32)[:, None] * inv_freq[None, :]
    angles = jnp.concatenate([angles, angles], axis=1)
    return (jnp.cos(angles), jnp.sin(angles))


def outer_rows(left, right):
    return lax.dot_general(
        left, right, (((1,), (1,)), ((), ())), preferred_element_type=jnp.float32
    )


def attention_kernel(
    heads, query_ref, key_ref, value_ref, grad_ref, cos_ref, sine_ref, out_ref, dquery_ref, dkv_ref
):
    seq_len, head_width = key_ref.shape
    score_scale = 1.0 / math.sqrt(head_width)
    cos_table, sine_table = cos_ref[...], sine_ref[...]

    def turned(features):
        return pltpu.roll(features, head_width // 2, 1) * sine_table

    def product(left, right, left_dim, right_dim):
        return lax.dot_general(
            left, right, (((left_dim,), (right_dim,)), ((), ())), preferred_element_type=jnp.float32
        )

    key_float = key_ref[...].astype(jnp.float32)
    key_rot = (key_float * cos_table + turned(key_float)).astype(jnp.bfloat16)
    value_part = value_ref[...]
    allowed = lax.broadcasted_iota(jnp.int32, (seq_len, seq_len), 1) <= lax.broadcasted_iota(
        jnp.int32, (seq_len, seq_len), 0
    )
    key_grad = jnp.zeros((seq_len, head_width), jnp.float32)
    value_grad = jnp.zeros((seq_len, head_width), jnp.float32)
    for head in range(heads):
        columns = slice(head * head_width, (head + 1) * head_width)
        query_float = query_ref[:, columns].astype(jnp.float32)
        query_rot = (query_float * cos_table + turned(query_float)).astype(jnp.bfloat16)
        grad_out = grad_ref[:, columns]
        logits = product(query_rot, key_rot, 1, 1) * score_scale
        logits = jnp.where(allowed, logits, -jnp.inf)
        raised = jnp.exp(logits - jnp.max(logits, axis=1, keepdims=True))
        attn_probs = raised * (1.0 / jnp.sum(raised, axis=1, keepdims=True))
        probs_low = attn_probs.astype(jnp.bfloat16)
        out_ref[:, columns] = product(probs_low, value_part, 1, 0).astype(jnp.bfloat16)
        prob_grad = product(grad_out, value_part, 1, 1)
        row_delta = jnp.sum(attn_probs * prob_grad, axis=1, keepdims=True)
        logit_grad = (attn_probs * (prob_grad - row_delta) * score_scale).astype(jnp.bfloat16)
        dquery = product(logit_grad, key_rot, 1, 0)
        dquery_ref[:, columns] = (dquery * cos_table - turned(dquery)).astype(jnp.bfloat16)
        key_grad = key_grad + product(logit_grad, query_rot, 0, 0)
        value_grad = value_grad + product(probs_low, grad_out, 0, 0)
    dkv_ref[:, :head_width] = (key_grad * cos_table - turned(key_grad)).astype(jnp.bfloat16)
    dkv_ref[:, head_width:] = value_grad.astype(jnp.bfloat16)


def attention(queries, key_rows, value_rows, grad_attn):
    tok_rows, width = queries.shape
    kv_local = key_rows.shape[1] // HD
    heads = width // HD // kv_local
    cos_table, sine_table = rotation(LEN, HD)
    sign = jnp.where(jnp.arange(HD) < HD // 2, -1.0, 1.0)[None, :]
    wide = pl.BlockSpec((LEN, heads * HD), lambda seq, head: (seq, head))
    narrow = pl.BlockSpec((LEN, HD), lambda seq, head: (seq, head))
    table = pl.BlockSpec((LEN, HD), lambda seq, head: (0, 0))
    pairs = tok_rows * LEN * (width // HD)
    return pl.pallas_call(
        functools.partial(attention_kernel, heads),
        grid=(tok_rows // LEN, kv_local),
        in_specs=[wide, narrow, narrow, wide, table, table],
        out_specs=[wide, wide, pl.BlockSpec((LEN, 2 * HD), lambda seq, head: (seq, head))],
        out_shape=[
            jax.ShapeDtypeStruct((tok_rows, width), jnp.bfloat16),
            jax.ShapeDtypeStruct((tok_rows, width), jnp.bfloat16),
            jax.ShapeDtypeStruct((tok_rows, 2 * kv_local * HD), jnp.bfloat16),
        ],
        compiler_params=pltpu.CompilerParams(vmem_limit_bytes=32 * 1024 * 1024),
        cost_estimate=pl.CostEstimate(
            flops=12 * pairs * HD, bytes_accessed=10 * tok_rows * width, transcendentals=pairs
        ),
    )(queries, key_rows, value_rows, grad_attn, cos_table, sine_table * sign)


def unfold_kernel(joined_ref, late_ref):
    share, col_share = joined_ref.shape[0], late_ref.shape[1]
    for owner in range(late_ref.shape[0] // share):
        late_ref[owner * share : (owner + 1) * share, :] = joined_ref[
            :, owner * col_share : (owner + 1) * col_share
        ]


def unfold(joined, head_rows, share, width):
    n_dp = lax.axis_size("dp")
    col_share = joined.shape[1] // n_dp
    first = head_rows // share
    return pl.pallas_call(
        unfold_kernel,
        grid=(width // col_share,),
        in_specs=[pl.BlockSpec((share, joined.shape[1]), lambda block: (first + block, 0))],
        out_specs=pl.BlockSpec((n_dp * share, col_share), lambda block: (0, block)),
        out_shape=jax.ShapeDtypeStruct((n_dp * share, width), joined.dtype),
        compiler_params=pltpu.CompilerParams(vmem_limit_bytes=16 * 1024 * 1024),
        cost_estimate=pl.CostEstimate(
            flops=0, bytes_accessed=4 * n_dp * share * width, transcendentals=0
        ),
    )(joined)


def exchange(parts, count):
    width = parts.shape[1] // count
    me = lax.axis_index("tensor")
    total = lax.dynamic_slice_in_dim(parts, me * width, width, 1).astype(jnp.float32)
    for step in range(1, count):
        target = lax.rem(me + step, count)
        sent = lax.dynamic_slice_in_dim(parts, target * width, width, 1)
        pairs = [(src, (src + step) % count) for src in range(count)]
        total = total + lax.ppermute(sent, "tensor", pairs).astype(jnp.float32)
    return total


def shards(
    cand_ids,
    val_ids,
    inputs,
    cotangent,
    queries,
    key_rows,
    value_rows,
    out_weight,
    val_inputs,
    val_cotangents,
    val_attention,
    val_query_grads,
    val_keyvalue_grads,
):
    tok_rows = cotangent.shape[0]
    seq_count = tok_rows // LEN
    live_rows = (cand_ids != pad_token).astype(jnp.float32)[:, None]
    val_live = (val_ids != pad_token).astype(jnp.float32)[:, None]

    def val_masked(rows):
        return (rows.astype(jnp.float32) * val_live).astype(jnp.bfloat16)

    late_rows = jnp.concatenate(
        [val_masked(val_query_grads), val_masked(val_keyvalue_grads)], axis=1
    )
    head_rows, col_share = out_weight.shape
    val_share, late_width = late_rows.shape
    late_blocks = late_rows.reshape(val_share, late_width // col_share, col_share).swapaxes(0, 1)
    joined = lax.all_gather(
        jnp.concatenate([out_weight, late_blocks.reshape(-1, col_share)], axis=0),
        "dp", axis=1, tiled=True,
    )
    early_rows = jnp.concatenate([val_attention, val_masked(val_cotangents), val_inputs], axis=1)
    masked = (cotangent.astype(jnp.float32) * live_rows).astype(jnp.bfloat16)
    joined, early_rows, masked = lax.optimization_barrier((joined, early_rows, masked))
    early = lax.all_gather(early_rows, "dp", axis=0, tiled=True)
    grad_attn = outer_rows(masked, joined[:head_rows]).astype(jnp.bfloat16)
    attended, dquery, kv_grads = attention(queries, key_rows, value_rows, grad_attn)
    late = unfold(joined, head_rows, val_share, late_width)
    feat_block = val_cotangents.shape[1]
    own_cotangent = lax.dynamic_slice_in_dim(
        masked, lax.axis_index("tensor") * feat_block, feat_block, 1
    )
    n_tensor = lax.axis_size("tensor")
    gram_proj = outer_rows(dquery, late[:, :feat_block]) + outer_rows(
        kv_grads, late[:, feat_block:]
    )
    gram_proj = gram_proj.astype(jnp.bfloat16)
    early, gram_proj = lax.optimization_barrier((early, gram_proj))
    share_proj = exchange(gram_proj, n_tensor)
    grams = [
        exchange(outer_rows(left, early[:, at * feat_block : (at + 1) * feat_block]).astype(jnp.bfloat16), n_tensor)
        for at, left in enumerate((attended, own_cotangent, inputs))
    ]
    factor = 1.0 / (64.0 * D)
    product = grams[0] * grams[1] + grams[2] * share_proj
    col_width = product.shape[1]
    by_seq = jnp.sum(product.reshape(seq_count, LEN, col_width), axis=1)
    column = lax.axis_index("tensor") * col_width + jnp.arange(col_width)
    member = ((column // LEN)[:, None] == jnp.arange(VALS)[None, :]).astype(jnp.float32)
    partial_scores = jnp.sum(by_seq[:, :, None] * member[None, :, :], axis=1)
    return lax.psum(partial_scores, "tensor") * factor


def solution(mesh):
    return jax.shard_map(
        shards,
        mesh=mesh,
        in_specs=(
            P("dp"),
            P("dp"),
            P("dp", "tensor"),
            P("dp", None),
            P("dp", "tensor"),
            P("dp", "tensor"),
            P("dp", "tensor"),
            P("tensor", "dp"),
            P("dp", "tensor"),
            P("dp", "tensor"),
            P("dp", "tensor"),
            P("dp", "tensor"),
            P("dp", "tensor"),
        ),
        out_specs=P("dp", None),
        check_vma=False,
    )
```

time: 604 us -> 598 us (0.990); the launches traced: 596 us -> 597 us
  waiting for transfers between devices: 292 us -> 411 us
  matrix products: 162 us -> 74.8 us
  local copies, waits for them, and re-layouts: 75.1 us -> 15.2 us
  Pallas kernels: 0 us -> 48.1 us
  other arithmetic: 45 us -> 24.8 us
    all_gather x2 -> x1, waiting for transfers between devices: 280 us -> 364 us  [shards(): lax.all_gather(jnp.concatenate([out_weight, late_blocks.reshape(-1, col_s...]
    dot_general x5 -> x0, matrix products: 74.4 us -> none  [the longest x1 27.6 us: attend_back(): jnp.einsum('skglm,smkd->slkgd', logit_grad, key_rot, preferred_element_ty...]
    pallas_call x0 -> x2, Pallas kernels: none -> 48.1 us  [the longest x1 40.5 us: attention(): pl.pallas_call(functools.partial(attention_kernel, heads), grid=(tok_rows...]
    convert_element_type x6 -> x0, local copies, waits for them, and re-layouts: 41.2 us -> none  [the longest x1 15.2 us: attend(): probs_low = attn_probs.astype(jnp.bfloat16)]
    all_gather x1, waiting for transfers between devices: 0.01 us -> 23.2 us  [shards(): early = lax.all_gather(early_rows, 'dp', axis=0, tiled=True)]
    reshape x4 -> x1, local copies, waits for them, and re-layouts: 16.4 us -> 0.39 us  [shards(): late_rows.reshape(val_share, late_width // col_share, col_share)]
    convert_element_type x4 -> x0, other arithmetic: 14.2 us -> none  [the longest x1 7.13 us: attend(): probs_low = attn_probs.astype(jnp.bfloat16)]
    ppermute x2 -> x4, waiting for transfers between devices: 10.6 us -> 24 us  [exchange(): total = total + lax.ppermute(sent, 'tensor', pairs).astype(jnp.float32)]
  transfers between devices with their start and end apart: 5 -> 6, of which waited for: 3 -> 5; matrix products, arithmetic and copies ran while one was open for 46% -> 14% of each run, Pallas kernels for 0% -> 8%
where the time goes in v2:
time: 598 us; the launch traced here: 597 us
  waiting for transfers between devices  411 us (69%)
  matrix products  74.8 us (13%)
  Pallas kernels  48.1 us (8%)
  other arithmetic  24.8 us (4%)
  local copies, waits for them, and re-layouts  15.2 us (3%)
  between operations  13.6 us (2%)
    all_gather x1, waiting for transfers between devices, shards(): lax.all_gather(jnp.concatenate([out_weight, late_blocks.reshape(-1, col_s...  364 us
    dot_general x6, matrix products, outer_rows(): lax.dot_general(left, right, (((1,), (1,)), ((), ())), preferred_element_...  74.8 us
    pallas_call x1, Pallas kernels, attention(): pl.pallas_call(functools.partial(attention_kernel, heads), grid=(tok_rows...  40.5 us
    ppermute x4, waiting for transfers between devices, exchange(): total = total + lax.ppermute(sent, 'tensor', pairs).astype(jnp.float32)  24 us
    all_gather x1, waiting for transfers between devices, shards(): early = lax.all_gather(early_rows, 'dp', axis=0, tiled=True)  23.2 us
  transfers between devices with their start and end apart: 6, of which 5 were waited for; matrix products, arithmetic and copies ran while one was open for 14% of the time, Pallas kernels for 8%

profile of v2, /device:TPU:0, one launch (start us, length us, event | category | flops | bytes accessed | tf_op | source)
XLA Modules:
  0.0 597.1 jit_solution(12319508816030186011)
XLA Ops:
  7.2 1.0 multiply_convert_fusion.3
  8.2 1.5 multiply_convert_fusion.1
  10.5 4.9 pad_maximum_fusion
  16.6 1.3 pad_maximum_fusion.1
  17.8 11.8 %multiply_convert_fusion = bf16[512,8192]{1,0:T(8,128)(2,1)} fusion(bf16[512,8192]{1,0:T(8,128)(2,1)} %param.16, f32[512]{0:T(512)S(1)} %compare_convert_fusion), kind=kLoop, calls=%fused_computation.2 | loop fusion | flops 12582912 | bytes 16779264 | tf_op jit(solution)/shard_map/convert_element_type | solution.py:180
  29.7 364.1 %all-gather.3.cloned.1.call-done.joined_ref = bf16[4736,8192]{1,0:T(8,128)(2,1)} async-done(((bf16[4736,512]{1,0:T(8,128)(2,1)}), bf16[4736,8192]{1,0:T(8,128)(2,1)}) %all-gather.3.cloned.1.call-update) | async-done | bytes 77594640 | tf_op jit(solution)/shard_map/all_gather | solution.py:175
  394.5 7.6 %shard_map.128 = bf16[1024,5120]{1,0:T(8,128)(2,1)S(1)} custom-call(bf16[4736,8192]{1,0:T(8,128)(2,1)} %all-gather.3.cloned.1.call-done.joined_ref), custom_call_target="tpu_custom_call" | custom-call | bytes 20971520 | tf_op jit(solution)/shard_map/pallas_call | solution.py:121
  402.0 3.9 copy-done
  405.9 43.2 %fusion.10.grad_ref = bf16[512,4096]{1,0:T(8,128)(2,1)} fusion(bf16[512,8192]{1,0:T(8,128)(2,1)} %multiply_convert_fusion, bf16[4736,8192]{1,0:T(8,128)(2,1)} %all-gather.3.cloned.1.call-done.joined_ref), kind=kOutput, calls=%fused_computation.11 | convolution fusion | flops 34361835520 | bytes 79691776 | tf_op jit(solution)/shard_map/dot_general | solution.py:32
  449.1 2.2 copy-done.2
  451.3 2.3 copy-done.6
  453.6 40.5 %shard_map.127 = (bf16[512,4096]{1,0:T(8,128)(2,1)S(1)}, bf16[512,4096]{1,0:T(8,128)(2,1)S(1)}, bf16[512,1024]{1,0:T(8,128)(2,1)S(1)}) custom-call(bf16[512,4096]{1,0:T(8,128)(2,1)S(1)} %copy-done.2, bf16[512,512]{1,0:T(8,128)(2,1)S(1)} %copy-done.3, bf16[512,512]{1,0:T(8,128)(2,1)S(1)} %copy-done.4, bf16[512,4096]{1,0:T(8,128)(2,1)S(1)} %copy-done.6, ...), custom_call_target="tpu_custom_call" | custom-call | flops 6442450944 | bytes 20971520 | tf_op jit(solution)/shard_map/pallas_call | solution.py:92
  494.1 1.3 fusion.14
  496.0 4.7 add_convert_fusion
  500.7 23.2 %all-gather.5.cloned.1.call-done = bf16[1024,12288]{1,0:T(8,128)(2,1)} async-done(((bf16[64,12288]{1,0:T(8,128)(2,1)}), bf16[1024,12288]{1,0:T(8,128)(2,1)}) %all-gather.5.cloned.1.call-update) | async-done | bytes 25165840 | tf_op jit(solution)/shard_map/all_gather | solution.py:182
  523.9 9.2 %fusion.18 = bf16[512,1024]{1,0:T(8,128)(2,1)S(1)} fusion(bf16[512,4096]{1,0:T(8,128)(2,1)} %copy-done.5, bf16[1024,12288]{1,0:T(8,128)(2,1)} %all-gather.5.cloned.1.call-done), kind=kOutput, calls=%fused_computation.18 | convolution fusion | flops 4295491584 | bytes 13631488 | tf_op jit(solution)/shard_map/dot_general | solution.py:32
  533.1 0.8 constant_dynamic-slice_fusion.2
  534.0 1.5 collective-permute-start
  535.4 9.4 %fusion.21 = bf16[512,1024]{1,0:T(8,128)(2,1)S(1)} fusion(bf16[1024,12288]{1,0:T(8,128)(2,1)} %all-gather.5.cloned.1.call-done, bf16[512,8192]{1,0:T(8,128)(2,1)} %multiply_convert_fusion, s32[]{:T(128)S(6)} %select_n.35), kind=kOutput, calls=%fused_computation.19 | convolution fusion | flops 4295491584 | bytes 13631492 | tf_op jit(solution)/shard_map/dot_general | solution.py:32
  544.8 0.9 constant_dynamic-slice_fusion
  545.7 0.8 collective-permute-start.1
  546.5 7.1 %fusion.26 = bf16[1024,512]{0,1:T(8,128)(2,1)S(1)} fusion(bf16[512,4096]{1,0:T(8,128)(2,1)S(1)} %copy-done.11, bf16[1024,12288]{1,0:T(8,128)(2,1)} %all-gather.5.cloned.1.call-done), kind=kOutput, calls=%fused_computation.20 | convolution fusion | flops 4295491584 | bytes 13631488 | tf_op jit(solution)/shard_map/dot_general | solution.py:32
  553.6 1.0 copy-done.7
  554.6 0.8 dynamic-slice_bitcast_fusion
  555.4 1.2 collective-permute-start.2
  556.6 0.8 constant_dynamic-slice_fusion.1
  557.5 0.8 collective-permute-start.3
  558.3 2.5 collective-permute-done.1
  560.8 11.2 %collective-permute-done.2 = bf16[512,512]{1,0:T(8,128)(2,1)} collective-permute-done((bf16[512,512]{1,0:T(8,128)(2,1)}, bf16[512,512]{1,0:T(8,128)(2,1)}, u32[]{:S(2)}, u32[]{:S(2)}) %collective-permute-start.2) | collective-permute-done | bytes 524320 | tf_op jit(solution)/shard_map/ppermute | solution.py:142
  572.0 10.3 %collective-permute-done.3 = bf16[512,512]{1,0:T(8,128)(2,1)} collective-permute-done((bf16[512,512]{1,0:T(8,128)(2,1)}, bf16[512,512]{1,0:T(8,128)(2,1)}, u32[]{:S(2)}, u32[]{:S(2)}) %collective-permute-start.3) | collective-permute-done | bytes 524320 | tf_op jit(solution)/shard_map/ppermute | solution.py:142
  582.3 2.4 bitcast_reduce_fusion
  584.8 4.9 psum.7
  (39 shorter events, 4.7 us)
Async XLA Ops:
  6.5 387.2 %all-gather.3.cloned.1.call-start = ((), (), s32[]{:S(2)}) async-start(), calls=%async_computation | async-start | bytes 82444288 | tf_op jit(solution)/shard_map/all_gather | solution.py:175
  15.3 0.7 copy-start.10
  15.3 1.1 copy-start.8
  15.4 1.2 copy-start.9
  15.4 508.6 %all-gather.5.cloned.1.call-start = ((), (), s32[]{:S(2)}) async-start(), calls=%async_computation.1 | async-start | bytes 26738688 | tf_op jit(solution)/shard_map/all_gather | solution.py:182
  402.0 3.9 copy-start
  405.9 43.2 %copy-start.3 = (bf16[512,512]{1,0:T(8,128)(2,1)S(1)}, bf16[512,512]{1,0:T(8,128)(2,1)}, u32[]{:S(2)}) copy-start(bf16[512,512]{1,0:T(8,128)(2,1)} %key_ref.1) | copy-start | bytes 1572868
  405.9 43.2 %copy-start.4 = (bf16[512,512]{1,0:T(8,128)(2,1)S(1)}, bf16[512,512]{1,0:T(8,128)(2,1)}, u32[]{:S(2)}) copy-start(bf16[512,512]{1,0:T(8,128)(2,1)} %value_ref.1) | copy-start | bytes 1572868
  449.1 2.2 copy-start.2
  451.3 2.3 copy-start.6
  453.6 40.5 %copy-start.1 = (bf16[1024,5120]{1,0:T(8,128)(2,1)S(1)}, bf16[1024,5120]{1,0:T(8,128)(2,1)}, u32[]{:S(2)}) copy-start(bf16[1024,5120]{1,0:T(8,128)(2,1)} %copy-done) | copy-start | bytes 31457284
  494.1 2.0 copy-start.5
  534.0 12.6 %copy-start.11 = (bf16[512,4096]{1,0:T(8,128)(2,1)S(1)}, bf16[512,4096]{1,0:T(8,128)(2,1)}, u32[]{:S(2)}) copy-start(bf16[512,4096]{1,0:T(8,128)(2,1)} %param.15) | copy-start | bytes 12582916
  534.0 24.4 %collective-permute-start = (bf16[512,512]{1,0:T(8,128)(2,1)}, bf16[512,512]{1,0:T(8,128)(2,1)}, u32[]{:S(2)}, u32[]{:S(2)}) collective-permute-start(bf16[512,512]{1,0:T(8,128)(2,1)} %constant_dynamic-slice_fusion.2), channel_id=1, source_target_pairs={{0,1},{1,0},{2,3},{3,2},{4,5},{5,4},{6,7},{7,6},{8,9},{9,8},{10,11... | collective-permute-start | bytes 1572872 | tf_op jit(solution)/shard_map/ppermute | solution.py:142
  545.7 15.1 %collective-permute-start.1 = (bf16[512,512]{1,0:T(8,128)(2,1)}, bf16[512,512]{1,0:T(8,128)(2,1)}, u32[]{:S(2)}, u32[]{:S(2)}) collective-permute-start(bf16[512,512]{1,0:T(8,128)(2,1)} %constant_dynamic-slice_fusion), channel_id=1, source_target_pairs={{0,1},{1,0},{2,3},{3,2},{4,5},{5,4},{6,7},{7,6},{8,9},{9,8},{10,11... | collective-permute-start | bytes 1572872 | tf_op jit(solution)/shard_map/ppermute | solution.py:142
  553.6 1.0 copy-start.7
  555.4 16.6 %collective-permute-start.2 = (bf16[512,512]{1,0:T(8,128)(2,1)}, bf16[512,512]{1,0:T(8,128)(2,1)}, u32[]{:S(2)}, u32[]{:S(2)}) collective-permute-start(bf16[512,512]{1,0:T(8,128)(2,1)} %dynamic-slice_bitcast_fusion), channel_id=1, source_target_pairs={{0,1},{1,0},{2,3},{3,2},{4,5},{5,4},{6,7},{7,6},{8,9},{9,8},{10,11... | collective-permute-start | bytes 1572872 | tf_op jit(solution)/shard_map/ppermute | solution.py:142
  557.5 24.9 %collective-permute-start.3 = (bf16[512,512]{1,0:T(8,128)(2,1)}, bf16[512,512]{1,0:T(8,128)(2,1)}, u32[]{:S(2)}, u32[]{:S(2)}) collective-permute-start(bf16[512,512]{1,0:T(8,128)(2,1)} %constant_dynamic-slice_fusion.1), channel_id=1, source_target_pairs={{0,1},{1,0},{2,3},{3,2},{4,5},{5,4},{6,7},{7,6},{8,9},{9,8},{10,11... | collective-permute-start | bytes 1572872 | tf_op jit(solution)/shard_map/ppermute | solution.py:142
Sparse Core Ops, SparseCore 0:
  15.5 378.1 all-gather.2
  395.3 128.5 all-gather.4
